TPU v7x, 256 devices: a whole 4x4x8 slice. The times are simulated.
256 devices in a mesh: section: 4 (over x_lo, core), expert: 64 (over x_hi, z, y).
Axes of the slice: x: 4 (x_hi: 2, x_lo: 2; x = x_hi * 2 + x_lo), y: 4, z: 8, core: 2. Of those that a mesh axis runs over, the one named last changes fastest.
Arguments:
- hidden_in: bfloat16 [1, 256, 3584], P(None, 'expert'), may hold values from -6 to 6
- routes: int32 [2, 4, 1, 256, 2], P(None, 'section', None, 'expert'), may hold values from 0 to 7, all different within a row; in each aligned block of 4 rows (0 to 3, 4 to 7, ..., all dimensions but the last counted through in order) at most 2 rows name the same one
- norm_gain: float32 [2, 4, 3584], P(None, 'section'), may hold values from 0.5 to 1.5
- router_weight: bfloat16 [2, 4, 3584, 8], P(None, 'section'), may hold values from -0.09375 to 0.09375
- gate_weight: bfloat16 [2, 4, 64, 3584, 256], P(None, 'section', 'expert'), may hold values from -0.09375 to 0.09375
- up_weight: bfloat16 [2, 4, 64, 3584, 256], P(None, 'section', 'expert'), may hold values from -0.09375 to 0.09375
- down_weight: bfloat16 [2, 4, 64, 256, 3584], P(None, 'section', 'expert'), may hold values from -0.125 to 0.125
Outputs:
- hidden_out: bfloat16 [1, 256, 3584], P(None, 'expert', 'section')
Inputs may be any that keep to these rules, and one draw needn't show every extreme that they name: `routes`: each row names 2 different experts. Among the 4 tokens of one block, for one layer and micro-batch, no expert is named more than 2 times, a bound that some block reaches.
All inputs are finite; a program needn't handle non-finite values.
Results may differ from a plain program's by a relative error of at most 0.04.
Values may be sent and summed in bfloat16 or wider, within the bound.
A program may use at most 64 MiB of HBM per device.

v0:
```python
import jax
import jax.numpy as jnp
from jax import lax
from jax.sharding import PartitionSpec as P


def passed_along(x, axis, by):
    peers = lax.axis_size(axis)
    pairs = [(i, i + by) for i in range(peers) if 0 <= i + by < peers]
    return lax.ppermute(x, axis, pairs)


def finish_rows(arrived, w_gate, w_up, w_down):
    lane_count, device_count, slot_count, model_width = arrived.shape
    flat_rows = arrived.reshape(lane_count, device_count * slot_count, model_width)
    gate_acts = jnp.einsum("lrd,ldh->lrh", flat_rows, w_gate, preferred_element_type=jnp.float32)
    up_acts = jnp.einsum("lrd,ldh->lrh", flat_rows, w_up, preferred_element_type=jnp.float32)
    hidden_acts = (jax.nn.silu(gate_acts) * up_acts).astype(jnp.bfloat16)
    partial_out = jnp.einsum(
        "lrh,lhd->lrd", hidden_acts, w_down, preferred_element_type=jnp.float32
    ).astype(jnp.bfloat16)
    partial_out = partial_out.reshape(lane_count, device_count, slot_count, model_width)
    return lax.all_to_all(partial_out, "expert", split_axis=1, concat_axis=1, tiled=True)


def lane_layer(lane_inputs, lane_gains, lane_routers, w_gate, w_up, w_down, lane_routes):
    lane_count, tok_rows, model_width = lane_inputs.shape
    expert_count = lane_routers.shape[-1]
    top_count = lane_routes.shape[-1]
    expert_devices = lax.axis_size("expert")
    slice_count = expert_devices // expert_count
    capacity = tok_rows * top_count // expert_count + 1
    widened = lane_inputs.astype(jnp.float32)
    mean_square = jnp.mean(widened * widened, axis=-1, keepdims=True)
    normalized = (widened * lax.rsqrt(mean_square + 1e-06) * lane_gains[:, None, :]).astype(
        jnp.bfloat16
    )
    router_logits = jnp.einsum(
        "ltd,lde->lte", normalized, lane_routers, preferred_element_type=jnp.float32
    )
    affinity = jax.nn.sigmoid(router_logits)
    expert_ids = jnp.arange(expert_count, dtype=jnp.int32)
    picked_onehot = (lane_routes[..., None] == expert_ids).astype(jnp.int32)
    chosen_affinity = jnp.sum(picked_onehot.astype(jnp.float32) * affinity[:, :, None, :], axis=-1)
    mix_weights = 2.5 * chosen_affinity / jnp.sum(chosen_affinity, axis=-1, keepdims=True)
    flat_onehot = picked_onehot.reshape(lane_count, tok_rows * top_count, expert_count)
    earlier_count = jnp.cumsum(flat_onehot, axis=1) - flat_onehot
    slot_index = jnp.sum(earlier_count * flat_onehot, axis=-1)
    buffer_pos = lane_routes.reshape(lane_count, tok_rows * top_count) * capacity + slot_index
    slot_ids = jnp.arange(expert_count * capacity, dtype=jnp.int32)
    slot_select = (buffer_pos[..., None] == slot_ids).astype(jnp.float32)
    slot_select = slot_select.reshape(lane_count, tok_rows, top_count, expert_count * capacity)
    place_matrix = jnp.sum(slot_select, axis=2).astype(jnp.bfloat16)
    mix_matrix = jnp.sum(slot_select * mix_weights[..., None], axis=2)
    outgoing = jnp.einsum(
        "ltp,ltd->lpd", place_matrix, normalized, preferred_element_type=jnp.float32
    ).astype(jnp.bfloat16)
    outgoing = outgoing.reshape(lane_count, expert_count, 1, capacity, model_width)
    outgoing = jnp.broadcast_to(
        outgoing, (lane_count, expert_count, slice_count, capacity, model_width)
    )
    outgoing = outgoing.reshape(lane_count, expert_devices, capacity, model_width)
    returned = finish_rows(
        lax.all_to_all(outgoing, "expert", split_axis=1, concat_axis=1, tiled=True),
        w_gate,
        w_up,
        w_down,
    )
    expert_output = jnp.sum(
        returned.reshape(lane_count, expert_count, slice_count, capacity, model_width).astype(
            jnp.float32
        ),
        axis=2,
    )
    expert_output = expert_output.reshape(lane_count, expert_count * capacity, model_width)
    routed_sum = jnp.einsum(
        "ltp,lpd->ltd", mix_matrix, expert_output, precision=lax.Precision.HIGHEST
    )
    return (widened + routed_sum).astype(jnp.bfloat16)


def pass_on(down_out, up_out):
    down_next = passed_along(down_out, "section", 1)
    up_next = passed_along(up_out, "section", -1)
    return (down_next, up_next)


def shards(hidden_in, routes, norm_gain, router_weight, gate_weight, up_weight, down_weight):
    section_pos = lax.axis_index("section")
    section_count = lax.axis_size("section")
    micro_count = hidden_in.shape[0]
    local_routes = routes[:, 0]
    local_gains = norm_gain[:, 0]
    local_routers = router_weight[:, 0]
    local_gate = gate_weight[:, 0, 0]
    local_up = up_weight[:, 0, 0]
    local_down = down_weight[:, 0, 0]

    def layer_on(first, last, inputs, routes_now):
        return lane_layer(
            inputs,
            local_gains[first:last],
            local_routers[first:last],
            local_gate[first:last],
            local_up[first:last],
            local_down[first:last],
            routes_now,
        )

    def routes_for(half_index, micro_pos):
        return lax.dynamic_index_in_dim(local_routes[half_index], micro_pos, 0, keepdims=True)

    empty_rows = jnp.zeros(hidden_in.shape[1:], jnp.bfloat16)
    down_recv = empty_rows
    up_recv = empty_rows
    finished = [empty_rows]
    down_live = micro_count + section_count - 1
    delay = 2 * section_count - 2
    tick_count = micro_count + delay
    for tick_index in range(tick_count):
        entering = hidden_in[min(tick_index, micro_count - 1)]
        down_out = empty_rows
        if tick_index < down_live:
            down_input = jnp.where(section_pos == 0, entering, down_recv)
            down_micro = jnp.clip(tick_index - section_pos, 0, micro_count - 1)
            down_out = layer_on(0, 1, down_input[None], routes_for(0, down_micro))[0]
        up_out = empty_rows
        if tick_index >= section_count - 1:
            up_input = jnp.where(section_pos == section_count - 1, down_out, up_recv)
            up_micro = jnp.clip(tick_index - delay + section_pos, 0, micro_count - 1)
            up_out = layer_on(1, 2, up_input[None], routes_for(1, up_micro))[0]
        leaving = tick_index - delay
        if leaving >= 0:
            finished[leaving] = up_out
        if tick_index + 1 < tick_count:
            down_recv, up_recv = pass_on(down_out, up_out)
    stacked = jnp.stack(finished)
    model_width = stacked.shape[2]
    quarters = stacked.reshape(
        micro_count, stacked.shape[1], section_count, model_width // section_count
    )
    arrived = lax.all_to_all(quarters, "section", split_axis=2, concat_axis=2, tiled=True)
    return arrived[:, :, 0, :]


def solution(mesh):
    return jax.shard_map(
        shards,
        mesh=mesh,
        in_specs=(
            P(None, "expert", None),
            P(None, "section", None, "expert", None),
            P(None, "section", None),
            P(None, "section", None, None),
            P(None, "section", "expert", None, None),
            P(None, "section", "expert", None, None),
            P(None, "section", "expert", None, None),
        ),
        out_specs=P(None, "expert", "section"),
        check_vma=False,
    )
```

profile of v0, /device:TPU:1, one launch (start us, length us, event | category | flops | bytes accessed | tf_op | source)
XLA Modules:
  0.0 641.1 jit_solution(5222297862644982681)
XLA Ops:
  0.0 0.8 slice_reduce_fusion
  3.0 1.0 fusion.161
  5.8 39.3 %all_to_all.85 = bf16[1,64,2,3584]{3,2,0,1:T(2,128)(2,1)S(1)} all-to-all(bf16[1,64,2,3584]{3,2,0,1:T(2,128)(2,1)S(1)} %bitcast.239), channel_id=1, replica_groups=mesh['section'=4,'expert'=64] {'expert'}, dimensions={1} | all-to-all | bytes 1835008 | tf_op jit(solution)/shard_map/all_to_all | solution.py:64
  45.5 1.9 fusion.48
  47.4 3.2 convolution_convert_fusion.7
  51.0 30.3 %all_to_all.86 = bf16[1,64,2,3584]{3,2,0,1:T(2,128)(2,1)S(1)} all-to-all(bf16[1,64,2,3584]{3,2,0,1:T(2,128)(2,1)S(1)} %bitcast.231), channel_id=1, replica_groups=mesh['section'=4,'expert'=64] {'expert'}, dimensions={1} | all-to-all | bytes 1835008 | tf_op jit(solution)/shard_map/all_to_all | solution.py:23
  81.3 0.8 convert_reduce_fusion.7
  82.5 7.8 %collective-permute-start = (bf16[4,3584]{1,0:T(4,128)(2,1)S(1)}, bf16[4,3584]{1,0:T(4,128)(2,1)S(1)}, u32[]{:S(2)}, u32[]{:S(2)}) collective-permute-start(bf16[4,3584]{1,0:T(4,128)(2,1)S(1)} %fusion), channel_id=1, source_target_pairs={{0,64},{64,128},{128,192},{1,65},{65,129},{129,193},{2,66},{66,130... | collective-permute-start | bytes 86024 | tf_op jit(solution)/shard_map/ppermute | solution.py:10
  90.3 1.0 collective-permute-done
  92.3 31.8 %all_to_all.87 = bf16[1,64,2,3584]{3,2,0,1:T(2,128)(2,1)S(1)} all-to-all(bf16[1,64,2,3584]{3,2,0,1:T(2,128)(2,1)S(1)} %bitcast.241), channel_id=1, replica_groups=mesh['section'=4,'expert'=64] {'expert'}, dimensions={1} | all-to-all | bytes 1835008 | tf_op jit(solution)/shard_map/all_to_all | solution.py:64
  124.4 1.9 fusion.46
  126.3 3.2 convolution_convert_fusion.6
  129.6 1.3 reshape.2127
  130.8 6.5 %all-to-all-start.3 = ((bf16[1,64,2,3584]{3,2,0,1:T(2,128)(2,1)}), bf16[1,64,2,3584]{3,2,0,1:T(2,128)(2,1)S(1)}, u32[]{:S(2)}, u32[]{:S(2)}) async-start(bf16[1,64,2,3584]{3,2,0,1:T(2,128)(2,1)} %bitcast.11), calls=%async_computation.3 | async-start | bytes 1835008 | tf_op jit(solution)/shard_map/all_to_all | solution.py:23
  137.9 26.1 %all-to-all-done.3 = bf16[1,64,2,3584]{3,2,0,1:T(2,128)(2,1)S(1)} async-done(((bf16[1,64,2,3584]{3,2,0,1:T(2,128)(2,1)}), bf16[1,64,2,3584]{3,2,0,1:T(2,128)(2,1)S(1)}, u32[]{:S(2)}, u32[]{:S(2)}) %all-to-all-start.3) | async-done | bytes 917536 | tf_op jit(solution)/shard_map/all_to_all | solution.py:23
  165.1 2.4 collective-permute-start.1
  167.5 1.2 collective-permute-done.1
  169.7 31.7 %all_to_all.88 = bf16[1,64,2,3584]{3,2,0,1:T(2,128)(2,1)S(1)} all-to-all(bf16[1,64,2,3584]{3,2,0,1:T(2,128)(2,1)S(1)} %bitcast.242), channel_id=1, replica_groups=mesh['section'=4,'expert'=64] {'expert'}, dimensions={1} | all-to-all | bytes 1835008 | tf_op jit(solution)/shard_map/all_to_all | solution.py:64
  201.7 1.9 fusion.44
  203.6 3.2 convolution_convert_fusion.5
  206.9 1.3 reshape.2130
  208.2 7.2 %all-to-all-start.5 = ((bf16[1,64,2,3584]{3,2,0,1:T(2,128)(2,1)}), bf16[1,64,2,3584]{3,2,0,1:T(2,128)(2,1)S(1)}, u32[]{:S(2)}, u32[]{:S(2)}) async-start(bf16[1,64,2,3584]{3,2,0,1:T(2,128)(2,1)} %bitcast.14), calls=%async_computation.5 | async-start | bytes 1835008 | tf_op jit(solution)/shard_map/all_to_all | solution.py:23
  215.8 24.4 %all-to-all-done.5 = bf16[1,64,2,3584]{3,2,0,1:T(2,128)(2,1)S(1)} async-done(((bf16[1,64,2,3584]{3,2,0,1:T(2,128)(2,1)}), bf16[1,64,2,3584]{3,2,0,1:T(2,128)(2,1)S(1)}, u32[]{:S(2)}, u32[]{:S(2)}) %all-to-all-start.5) | async-done | bytes 917536 | tf_op jit(solution)/shard_map/all_to_all | solution.py:23
  241.4 2.9 collective-permute-start.2
  244.3 2.2 collective-permute-done.2
  247.4 31.4 %all_to_all.89 = bf16[1,64,2,3584]{3,2,0,1:T(2,128)(2,1)S(1)} all-to-all(bf16[1,64,2,3584]{3,2,0,1:T(2,128)(2,1)S(1)} %bitcast.243), channel_id=1, replica_groups=mesh['section'=4,'expert'=64] {'expert'}, dimensions={1} | all-to-all | bytes 1835008 | tf_op jit(solution)/shard_map/all_to_all | solution.py:64
  279.2 1.9 fusion.42
  281.2 3.2 convolution_convert_fusion.4
  284.4 1.3 reshape.2133
  285.7 7.2 %all-to-all-start.7 = ((bf16[1,64,2,3584]{3,2,0,1:T(2,128)(2,1)}), bf16[1,64,2,3584]{3,2,0,1:T(2,128)(2,1)S(1)}, u32[]{:S(2)}, u32[]{:S(2)}) async-start(bf16[1,64,2,3584]{3,2,0,1:T(2,128)(2,1)} %bitcast.17), calls=%async_computation.7 | async-start | bytes 1835008 | tf_op jit(solution)/shard_map/all_to_all | solution.py:23
  292.9 4.1 collective-permute-start.3
  297.5 20.1 %all-to-all-done.7 = bf16[1,64,2,3584]{3,2,0,1:T(2,128)(2,1)S(1)} async-done(((bf16[1,64,2,3584]{3,2,0,1:T(2,128)(2,1)}), bf16[1,64,2,3584]{3,2,0,1:T(2,128)(2,1)S(1)}, u32[]{:S(2)}, u32[]{:S(2)}) %all-to-all-start.7) | async-done | bytes 917536 | tf_op jit(solution)/shard_map/all_to_all | solution.py:23
  320.3 32.0 %all_to_all.90 = bf16[1,64,2,3584]{3,2,0,1:T(2,128)(2,1)S(1)} all-to-all(bf16[1,64,2,3584]{3,2,0,1:T(2,128)(2,1)S(1)} %bitcast.244), channel_id=1, replica_groups=mesh['section'=4,'expert'=64] {'expert'}, dimensions={1} | all-to-all | bytes 1835008 | tf_op jit(solution)/shard_map/all_to_all | solution.py:64
  352.6 1.9 fusion.28
  354.5 3.2 convolution_convert_fusion.3
  358.1 31.9 %all_to_all.91 = bf16[1,64,2,3584]{3,2,0,1:T(2,128)(2,1)S(1)} all-to-all(bf16[1,64,2,3584]{3,2,0,1:T(2,128)(2,1)S(1)} %bitcast.232), channel_id=1, replica_groups=mesh['section'=4,'expert'=64] {'expert'}, dimensions={1} | all-to-all | bytes 1835008 | tf_op jit(solution)/shard_map/all_to_all | solution.py:23
  391.2 5.5 collective-permute-start.4
  396.7 0.8 collective-permute-done.4
  398.5 32.4 %all_to_all.92 = bf16[1,64,2,3584]{3,2,0,1:T(2,128)(2,1)S(1)} all-to-all(bf16[1,64,2,3584]{3,2,0,1:T(2,128)(2,1)S(1)} %bitcast.246), channel_id=1, replica_groups=mesh['section'=4,'expert'=64] {'expert'}, dimensions={1} | all-to-all | bytes 1835008 | tf_op jit(solution)/shard_map/all_to_all | solution.py:64
  431.3 1.9 fusion.26
  433.2 3.2 convolution_convert_fusion.2
  436.4 1.3 reshape.2144
  437.7 7.3 %all-to-all-start.11 = ((bf16[1,64,2,3584]{3,2,0,1:T(2,128)(2,1)}), bf16[1,64,2,3584]{3,2,0,1:T(2,128)(2,1)S(1)}, u32[]{:S(2)}, u32[]{:S(2)}) async-start(bf16[1,64,2,3584]{3,2,0,1:T(2,128)(2,1)} %bitcast.28), calls=%async_computation.11 | async-start | bytes 1835008 | tf_op jit(solution)/shard_map/all_to_all | solution.py:23
  445.6 24.7 %all-to-all-done.11 = bf16[1,64,2,3584]{3,2,0,1:T(2,128)(2,1)S(1)} async-done(((bf16[1,64,2,3584]{3,2,0,1:T(2,128)(2,1)}), bf16[1,64,2,3584]{3,2,0,1:T(2,128)(2,1)S(1)}, u32[]{:S(2)}, u32[]{:S(2)}) %all-to-all-start.11) | async-done | bytes 917536 | tf_op jit(solution)/shard_map/all_to_all | solution.py:23
  470.2 0.8 convert_reduce_fusion.2
  471.4 4.5 collective-permute-start.5
  476.0 0.8 collective-permute-done.5
  477.8 34.5 %all_to_all.93 = bf16[1,64,2,3584]{3,2,0,1:T(2,128)(2,1)S(1)} all-to-all(bf16[1,64,2,3584]{3,2,0,1:T(2,128)(2,1)S(1)} %bitcast.247), channel_id=1, replica_groups=mesh['section'=4,'expert'=64] {'expert'}, dimensions={1} | all-to-all | bytes 1835008 | tf_op jit(solution)/shard_map/all_to_all | solution.py:64
  512.6 1.9 fusion.24
  514.5 3.2 convolution_convert_fusion.1
  517.8 1.3 reshape.2147
  519.0 6.2 all-to-all-start.13
  525.7 26.0 %all-to-all-done.13 = bf16[1,64,2,3584]{3,2,0,1:T(2,128)(2,1)S(1)} async-done(((bf16[1,64,2,3584]{3,2,0,1:T(2,128)(2,1)}), bf16[1,64,2,3584]{3,2,0,1:T(2,128)(2,1)S(1)}, u32[]{:S(2)}, u32[]{:S(2)}) %all-to-all-start.13) | async-done | bytes 917536 | tf_op jit(solution)/shard_map/all_to_all | solution.py:23
  551.8 0.8 convert_reduce_fusion.1
  553.0 3.6 collective-permute-start.6
  556.6 1.8 collective-permute-done.6
  559.3 33.2 %all_to_all.94 = bf16[1,64,2,3584]{3,2,0,1:T(2,128)(2,1)S(1)} all-to-all(bf16[1,64,2,3584]{3,2,0,1:T(2,128)(2,1)S(1)} %bitcast.248), channel_id=1, replica_groups=mesh['section'=4,'expert'=64] {'expert'}, dimensions={1} | all-to-all | bytes 1835008 | tf_op jit(solution)/shard_map/all_to_all | solution.py:64
  592.8 1.9 fusion.22
  594.8 3.2 convolution_convert_fusion
  598.0 1.3 reshape.2150
  599.3 6.1 all-to-all-start.15
  605.9 25.8 %all-to-all-done.15 = bf16[1,64,2,3584]{3,2,0,1:T(2,128)(2,1)S(1)} async-done(((bf16[1,64,2,3584]{3,2,0,1:T(2,128)(2,1)}), bf16[1,64,2,3584]{3,2,0,1:T(2,128)(2,1)S(1)}, u32[]{:S(2)}, u32[]{:S(2)}) %all-to-all-start.15) | async-done | bytes 917536 | tf_op jit(solution)/shard_map/all_to_all | solution.py:23
  631.7 0.8 convert_reduce_fusion
  632.9 7.4 %all_to_all.95 = bf16[1,4,4,896]{3,1,0,2:T(4,128)(2,1)S(1)} all-to-all(bf16[1,4,4,896]{3,1,0,2:T(4,128)(2,1)S(1)} %bitcast.249), channel_id=1, replica_groups=mesh['section'=4,'expert'=64] {'section'}, dimensions={2} | all-to-all | bytes 57344 | tf_op jit(solution)/shard_map/all_to_all | solution.py:142
  (123 shorter events, 24.4 us)
Async XLA Ops:
  51.0 31.2 %copy-start = (bf16[1,4,3584]{2,1,0:T(4,128)(2,1)S(1)}, bf16[1,4,3584]{2,1,0:T(4,128)(2,1)}, u32[]{:S(2)}) copy-start(bf16[1,4,3584]{2,1,0:T(4,128)(2,1)} %param.7) | copy-start | bytes 86020
  82.5 8.8 %collective-permute-start = (bf16[4,3584]{1,0:T(4,128)(2,1)S(1)}, bf16[4,3584]{1,0:T(4,128)(2,1)S(1)}, u32[]{:S(2)}, u32[]{:S(2)}) collective-permute-start(bf16[4,3584]{1,0:T(4,128)(2,1)S(1)} %fusion), channel_id=1, source_target_pairs={{0,64},{64,128},{128,192},{1,65},{65,129},{129,193},{2,66},{66,130... | collective-permute-start | bytes 86024 | tf_op jit(solution)/shard_map/ppermute | solution.py:10
  129.5 7.8 %copy-start.1 = (bf16[2,1,3584,8]{2,3,1,0:T(8,128)(2,1)S(1)}, bf16[2,1,3584,8]{2,3,1,0:T(8,128)(2,1)}, u32[]{:S(2)}) copy-start(bf16[2,1,3584,8]{2,3,1,0:T(8,128)(2,1)} %param.10) | copy-start | bytes 344068
  130.8 33.1 %all-to-all-start.3 = ((bf16[1,64,2,3584]{3,2,0,1:T(2,128)(2,1)}), bf16[1,64,2,3584]{3,2,0,1:T(2,128)(2,1)S(1)}, u32[]{:S(2)}, u32[]{:S(2)}) async-start(bf16[1,64,2,3584]{3,2,0,1:T(2,128)(2,1)} %bitcast.11), calls=%async_computation.3 | async-start | bytes 1835008 | tf_op jit(solution)/shard_map/all_to_all | solution.py:23
  165.1 3.6 collective-permute-start.1
  208.2 32.1 %all-to-all-start.5 = ((bf16[1,64,2,3584]{3,2,0,1:T(2,128)(2,1)}), bf16[1,64,2,3584]{3,2,0,1:T(2,128)(2,1)S(1)}, u32[]{:S(2)}, u32[]{:S(2)}) async-start(bf16[1,64,2,3584]{3,2,0,1:T(2,128)(2,1)} %bitcast.14), calls=%async_computation.5 | async-start | bytes 1835008 | tf_op jit(solution)/shard_map/all_to_all | solution.py:23
  241.4 5.1 collective-permute-start.2
  285.7 31.9 %all-to-all-start.7 = ((bf16[1,64,2,3584]{3,2,0,1:T(2,128)(2,1)}), bf16[1,64,2,3584]{3,2,0,1:T(2,128)(2,1)S(1)}, u32[]{:S(2)}, u32[]{:S(2)}) async-start(bf16[1,64,2,3584]{3,2,0,1:T(2,128)(2,1)} %bitcast.17), calls=%async_computation.7 | async-start | bytes 1835008 | tf_op jit(solution)/shard_map/all_to_all | solution.py:23
  292.9 25.7 %collective-permute-start.3 = (bf16[4,3584]{1,0:T(4,128)(2,1)S(1)}, bf16[4,3584]{1,0:T(4,128)(2,1)S(1)}, u32[]{:S(2)}, u32[]{:S(2)}) collective-permute-start(bf16[4,3584]{1,0:T(4,128)(2,1)S(1)} %broadcast_in_dim.52), channel_id=1, source_target_pairs={{64,0},{128,64},{192,128},{65,1},{129,65},{193,129},{66,2},{130,66... | collective-permute-start | bytes 86024 | tf_op jit(solution)/shard_map/ppermute | solution.py:10
  391.2 6.4 collective-permute-start.4
  437.7 32.5 %all-to-all-start.11 = ((bf16[1,64,2,3584]{3,2,0,1:T(2,128)(2,1)}), bf16[1,64,2,3584]{3,2,0,1:T(2,128)(2,1)S(1)}, u32[]{:S(2)}, u32[]{:S(2)}) async-start(bf16[1,64,2,3584]{3,2,0,1:T(2,128)(2,1)} %bitcast.28), calls=%async_computation.11 | async-start | bytes 1835008 | tf_op jit(solution)/shard_map/all_to_all | solution.py:23
  471.4 5.4 collective-permute-start.5
  519.0 32.7 %all-to-all-start.13 = ((bf16[1,64,2,3584]{3,2,0,1:T(2,128)(2,1)}), bf16[1,64,2,3584]{3,2,0,1:T(2,128)(2,1)S(1)}, u32[]{:S(2)}, u32[]{:S(2)}) async-start(bf16[1,64,2,3584]{3,2,0,1:T(2,128)(2,1)} %bitcast.31), calls=%async_computation.13 | async-start | bytes 1835008 | tf_op jit(solution)/shard_map/all_to_all | solution.py:23
  553.0 5.4 collective-permute-start.6
  599.3 32.5 %all-to-all-start.15 = ((bf16[1,64,2,3584]{3,2,0,1:T(2,128)(2,1)}), bf16[1,64,2,3584]{3,2,0,1:T(2,128)(2,1)S(1)}, u32[]{:S(2)}, u32[]{:S(2)}) async-start(bf16[1,64,2,3584]{3,2,0,1:T(2,128)(2,1)} %bitcast.34), calls=%async_computation.15 | async-start | bytes 1835008 | tf_op jit(solution)/shard_map/all_to_all | solution.py:23
where the time goes:
time: 651 us; the launch traced here: 641 us
  blocking collectives  336 us (52%)
  waiting for transfers between devices  155 us (24%)
  starting transfers between devices  71.3 us (11%)
  matrix products  47.7 us (7%)
  local copies, waits for them, and re-layouts  19.4 us (3%)
  other arithmetic  11.1 us (2%)
    all_to_all x8, blocking collectives, lane_layer(): lax.all_to_all(outgoing, 'expert', split_axis=1, concat_axis=1, tiled=True)  266 us
    all_to_all x6, waiting for transfers between devices, finish_rows(): lax.all_to_all(partial_out, 'expert', split_axis=1, concat_axis=1, tiled=...  147 us
    all_to_all x2, blocking collectives, finish_rows(): lax.all_to_all(partial_out, 'expert', split_axis=1, concat_axis=1, tiled=...  62.1 us
    all_to_all x6, starting transfers between devices, finish_rows(): lax.all_to_all(partial_out, 'expert', split_axis=1, concat_axis=1, tiled=...  40.4 us
    ppermute x7, starting transfers between devices, passed_along(): return lax.ppermute(x, axis, pairs)  30.9 us
    dot_general x8, matrix products, finish_rows(): jnp.einsum('lrh,lhd->lrd', hidden_acts, w_down, preferred_element_type=jn...  25.9 us
    dot_general x8, matrix products, finish_rows(): jnp.einsum('lrd,ldh->lrh', flat_rows, w_gate, preferred_element_type=jnp....  15.3 us
  transfers between devices with their start and end apart: 13, of which 12 were waited for; matrix products, arithmetic and copies ran while one was open for 1% of the time, Pallas kernels for 0%

commit v1 on v0

v1 whole, which is shorter than its diff:
```python
import functools

import jax
import jax.numpy as jnp
from jax import lax
from jax.experimental import pallas as pl
from jax.experimental.pallas import tpu as pltpu
from jax.sharding import PartitionSpec as P

MESH = pl.DeviceIdType.MESH
F32 = jnp.float32
BF16 = jnp.bfloat16

OWNER = 2
D = 3584
CH = 896
HID = 256
EXPERTS = 8
ROWS = 8
SET = 16
STEPS = 8
GROUPS = 4
PER = EXPERTS // GROUPS


def remote(src, dst, send, recv, section, expert):
    return pltpu.make_async_remote_copy(
        src_ref=src,
        dst_ref=dst,
        send_sem=send,
        recv_sem=recv,
        device_id=(section, expert),
        device_id_type=MESH,
    )


def wait_for(ref, sem):
    pltpu.make_async_copy(ref, ref, sem).wait()


def iota(shape, dim):
    return lax.broadcasted_iota(jnp.int32, shape, dim)


def kernel(
    hidden_hbm, routes_hbm, gain_hbm, router_hbm, gate_hbm, up_hbm, down_hbm, out_ref,
    hid_v, routes_v, gain_v, router_v, gate_v, up_v, down_v,
    rt_out, rt_in, rsum, hx_out, hx_in, pt, x_v, disp, xb, sb, rb, aff_v, pb, ro,
    fin_out, fin_in,
    in_sem, w_sem, rt_send, rt_recv, hx_send, hx_recv, d_send, d_recv, g_send, g_recv,
    r_send, r_recv, c_send, c_recv, f_send, f_recv,
):
    s = lax.axis_index("section")
    i = lax.axis_index("expert")
    xh = i // 32
    z = (i // 4) % 8
    y = i % 4
    zp = z % 2
    e = i // 8
    me8 = i % 8
    base8 = i - me8
    base4 = i - y
    is_owner = s == OWNER

    def y_at(k):
        return (y + k) % 4

    def member(zr, k):
        return ((zp + zr) % 2) * 4 + y_at(k)

    def to_live(j, xf):
        up = (z + j) % 2 == 0
        zd = jnp.where(up, (z + j) % 8, (z - j + 8) % 8)
        xd = (xh + xf) % 2
        return xd, zd

    def to_owner(j, xf):
        zo = jnp.where(zp == 0, (z - j + 8) % 8, (z + j) % 8)
        xd = (xh + xf) % 2
        return xd * 32 + zo * 4 + y

    small = [
        pltpu.make_async_copy(hidden_hbm, hid_v, in_sem.at[0]),
        pltpu.make_async_copy(routes_hbm, routes_v, in_sem.at[1]),
    ]
    for copy in small:
        copy.start()

    def weights(c):
        return [
            pltpu.make_async_copy(gain_hbm.at[c], gain_v.at[c], w_sem.at[c, 0]),
            pltpu.make_async_copy(router_hbm.at[c], router_v.at[c], w_sem.at[c, 1]),
            pltpu.make_async_copy(gate_hbm.at[c, 0, 0], gate_v.at[c], w_sem.at[c, 2]),
            pltpu.make_async_copy(up_hbm.at[c, 0, 0], up_v.at[c], w_sem.at[c, 3]),
            pltpu.make_async_copy(down_hbm.at[c, 0, 0], down_v.at[c], w_sem.at[c, 4]),
        ]

    for c in range(2):
        for copy in weights(c):
            copy.start()

    barrier = pltpu.get_barrier_semaphore()

    def greet(section, expert):
        pl.semaphore_signal(barrier, inc=1, device_id=(section, expert), device_id_type=MESH)

    for k in range(1, 8):
        greet(s, base8 + (me8 + k) % 8)
    for k in range(1, 4):
        greet(OWNER, base4 + y_at(k))
    for j in range(4):
        for xf in range(2):
            if j == 0 and xf == 0:
                @pl.when(jnp.logical_not(is_owner))
                def _():
                    greet(OWNER, to_owner(0, 0))
            else:
                greet(OWNER, to_owner(j, xf))

    @pl.when(is_owner)
    def _():
        for sec in range(4):
            for k in range(1, 4):
                greet(sec, base4 + y_at(k))
            for j in range(4):
                for xf in range(2):
                    if sec == OWNER and j == 0 and xf == 0:
                        continue
                    xd, zd = to_live(j, xf)
                    greet(sec, xd * 32 + zd * 4 + y)
        pl.semaphore_wait(barrier, 60)

    @pl.when(jnp.logical_not(is_owner))
    def _():
        pl.semaphore_wait(barrier, 18)

    for copy in small:
        copy.wait()
    place = (iota((SET, 4), 0) == 4 * y + iota((SET, 4), 1)).astype(BF16)
    lane = iota((4, 128), 1)
    tile = jnp.zeros((4, 128), F32)
    for c in range(2):
        chosen = routes_v[c, 0, 0].astype(F32)
        for k in range(2):
            tile = tile + jnp.where(lane == 2 * c + k, chosen[:, k : k + 1], 0.0)
    rt_out[...] = jnp.dot(place, tile.astype(BF16), preferred_element_type=F32)

    @pl.when(is_owner)
    def _():
        placed = jnp.dot(place, hid_v[0], preferred_element_type=F32).astype(BF16)
        for k in range(4):
            hx_out[k] = placed[:, k * CH : (k + 1) * CH]
        for k in range(1, 4):
            remote(
                hx_out.at[y_at(k)], hx_in.at[y], hx_send.at[k], hx_recv.at[y],
                s, base4 + y_at(k),
            ).start()

    for k in range(1, 4):
        remote(
            rt_out, rt_in.at[s, y], rt_send.at[k], rt_recv.at[s, y], OWNER, base4 + y_at(k)
        ).start()

    @pl.when(jnp.logical_not(is_owner))
    def _():
        remote(
            rt_out, rt_in.at[s, y], rt_send.at[0], rt_recv.at[s, y], OWNER, i
        ).start()

    def live_of(step):
        return jnp.where(step < 4, step, 7 - step)

    def make_pt(step):
        half = step // 4
        routes = rsum[live_of(step)]
        lanes = iota((SET, 128), 1)
        first = jnp.sum(jnp.where(lanes == 2 * half, routes, 0.0), axis=1, keepdims=True)
        second = jnp.sum(jnp.where(lanes == 2 * half + 1, routes, 0.0), axis=1, keepdims=True)
        slots = iota((SET, 64), 1)
        token = iota((SET, 64), 0)
        expert = (slots // 8).astype(F32)
        named = jnp.logical_or(first == expert, second == expert)
        onehot = jnp.where(named, 1.0, 0.0)
        row = iota((SET, SET), 0)
        col = iota((SET, SET), 1)
        earlier = jnp.logical_and(row // 4 == col // 4, col < row)
        count = jnp.dot(
            jnp.where(earlier, 1.0, 0.0).astype(BF16), onehot.astype(BF16),
            preferred_element_type=F32,
        )
        fits = jnp.logical_and(
            count == (slots % 2).astype(F32), (slots % 8) // 2 == token // 4
        )
        pt[step] = jnp.where(jnp.logical_and(named, fits), 1.0, 0.0).astype(BF16)

    @pl.when(is_owner)
    def _():
        rt_in[OWNER, y] = rt_out[...]
        for k in range(1, 4):
            wait_for(hx_in.at[y_at(k)], hx_recv.at[y_at(k)])
        hx_in[y] = hx_out[y]
        x = jnp.zeros((SET, CH), F32)
        for k in range(4):
            x = x + hx_in[k].astype(F32)
        x_v[...] = x
        for sec in range(4):
            for k in range(4):
                if k == 0 and sec == OWNER:
                    continue
                wait_for(rt_in.at[sec, y_at(k)], rt_recv.at[sec, y_at(k)])
            total = jnp.zeros((SET, 128), F32)
            for k in range(4):
                total = total + rt_in[sec, k]
            rsum[sec] = total
        make_pt(0)

    def combine(step):
        for k in range(EXPERTS):
            wait_for(ro.at[k], c_recv.at[k])
        rows = ro[...].astype(F32).reshape(EXPERTS * ROWS, CH + 128).astype(BF16)
        mixed = jnp.dot(pt[step], rows, preferred_element_type=F32)
        weight = mixed[:, CH : CH + 1] + mixed[:, CH + 1 : CH + 2]
        fresh = x_v[...] + 2.5 * mixed[:, :CH] / weight
        x_v[...] = fresh.astype(BF16).astype(F32)

    def owner_step(step):
        live = live_of(step)
        half = step // 4

        @pl.when(step > 0)
        def _():
            combine(step - 1)
            for m in range(1, 8):
                wait_for(disp.at[m], d_send.at[m])

            @pl.when(live_of(step - 1) != OWNER)
            def _():
                wait_for(disp.at[0], d_send.at[0])

        rows = lax.dot_general(
            pt[step], x_v[...].astype(BF16), (((0,), (0,)), ((), ())),
            preferred_element_type=F32,
        )
        disp[...] = rows.reshape(EXPERTS, ROWS, CH).astype(BF16)
        for j in (3, 2, 1, 0):
            for xf in (1, 0):
                m = 2 * j + xf
                xd, zd = to_live(j, xf)
                src = disp.at[xd * 4 + zd // 2]
                dst = xb.at[half, y, zd % 2, m]

                def send():
                    remote(
                        src, dst, d_send.at[m], d_recv.at[half, m], live, xd * 32 + zd * 4 + y
                    ).start()

                if m > 0:
                    send()
                else:
                    pl.when(live != OWNER)(send)

                    @pl.when(live == OWNER)
                    def _():
                        pltpu.make_async_copy(src, dst, d_recv.at[half, m]).start()

        @pl.when(step < STEPS - 1)
        def _():
            make_pt(step + 1)

    others = [(1, 2), (1, 1), (1, 3), (0, 2), (0, 1), (0, 3), (1, 0)]

    def live_step(half):
        for part in reversed(range(GROUPS)):
            for m in range(part * PER, (part + 1) * PER):
                wait_for(xb.at[half, y, zp, m], d_recv.at[half, m])
            rows = xb.at[half, y, zp, pl.ds(part * PER, PER)]
            for n, (zr, k) in enumerate(others):
                remote(
                    rows, rows, g_send.at[n, part], g_recv.at[half, me8, part],
                    s, base8 + member(zr, k),
                ).start()
        for copy in weights(half):
            copy.wait()
        gate = jnp.zeros((128, HID), F32)
        up = jnp.zeros((128, HID), F32)
        logits = jnp.zeros((128, EXPERTS), F32)
        squares = jnp.zeros((128, 1), F32)
        for k in (0, 1, 3, 2):
            yk = y_at(k)
            for zr in range(2):
                if zr == 0 and k == 0:
                    continue
                for part in range(GROUPS):
                    wait_for(
                        xb.at[half, yk, (zp + zr) % 2, pl.ds(part * PER, PER)],
                        g_recv.at[half, member(zr, k), part],
                    )
            rows = xb[half, yk].astype(F32).reshape(128, CH)
            squares = squares + jnp.sum(rows * rows, axis=1, keepdims=True)
            start = pl.multiple_of(yk * CH, 128)
            scaled = (rows * gain_v[half, :, pl.ds(start, CH)]).astype(BF16)
            depth = pl.ds(start, CH)
            gate = gate + jnp.dot(scaled, gate_v[half, depth, :], preferred_element_type=F32)
            up = up + jnp.dot(scaled, up_v[half, depth, :], preferred_element_type=F32)
            logits = logits + jnp.dot(
                scaled, router_v[half, 0, depth, :], preferred_element_type=F32
            )
        scale = lax.rsqrt(squares * (1.0 / D) + 1e-06)
        gate = gate * scale
        act = (gate * jax.nn.sigmoid(gate) * (up * scale)).astype(BF16)
        own = jnp.where(iota((128, EXPERTS), 1) == e, logits, 0.0)
        affinity = jax.nn.sigmoid(jnp.sum(own, axis=1, keepdims=True) * scale)
        aff_v[...] = jnp.broadcast_to(affinity, (128, 128))

        for k in (2, 1, 3, 0):
            yk = y_at(k)
            cols = pl.ds(pl.multiple_of(yk * CH, 128), CH)
            piece = jnp.dot(act, down_v[half, :, cols], preferred_element_type=F32)
            sb[yk] = piece.astype(BF16).reshape(2, 64, CH)
            for zr in (1, 0):
                if zr == 0 and k == 0:
                    continue
                n = others.index((zr, k))
                remote(
                    sb.at[yk, (zp + zr) % 2], rb.at[half, me8], r_send.at[n],
                    r_recv.at[half, me8], s, base8 + member(zr, k),
                ).start()
        total = sb[y, zp].astype(F32)
        for zr, k in reversed(others):
            src = member(zr, k)
            wait_for(rb.at[half, src], r_recv.at[half, src])
            total = total + rb[half, src].astype(F32)
        mine = aff_v[pl.ds(pl.multiple_of(zp * 64, 64), 64), :]
        pb[:, :, :CH] = (total * mine[:, :1]).reshape(EXPERTS, ROWS, CH).astype(BF16)
        high = mine.astype(BF16).astype(F32)
        lanes = iota((64, 128), 1)
        extra = jnp.where(lanes == 0, high, jnp.where(lanes == 1, mine - high, 0.0))
        pb[:, :, CH:] = extra.reshape(EXPERTS, ROWS, 128).astype(BF16)
        for j in (3, 2, 1, 0):
            for xf in (1, 0):
                m = 2 * j + xf

                def send():
                    remote(
                        pb.at[m], ro.at[e], c_send.at[m], c_recv.at[e], OWNER, to_owner(j, xf)
                    ).start()

                if m > 0:
                    send()
                else:
                    pl.when(jnp.logical_not(is_owner))(send)

                    @pl.when(is_owner)
                    def _():
                        pltpu.make_async_copy(pb.at[m], ro.at[e], c_recv.at[e]).start()

        for n, (zr, k) in enumerate(others):
            for part in range(GROUPS):
                wait_for(xb.at[half, y, zp, pl.ds(part * PER, PER)], g_send.at[n, part])
            wait_for(sb.at[0, 0], r_send.at[n])
        for m in range(1, 8):
            wait_for(pb.at[m], c_send.at[m])

        @pl.when(jnp.logical_not(is_owner))
        def _():
            wait_for(pb.at[0], c_send.at[0])

    def one_step(step, carry):
        pl.when(is_owner)(lambda: owner_step(step))
        pl.when(s == live_of(step))(lambda: live_step(step // 4))
        return carry

    lax.fori_loop(0, STEPS, one_step, 0)

    @pl.when(is_owner)
    def _():
        combine(STEPS - 1)
        for m in range(8):
            wait_for(disp.at[m], d_send.at[m])
        fin_out[...] = x_v[...].astype(BF16)
        for k in range(4):
            def send():
                remote(fin_out, fin_in, f_send.at[k], f_recv, y, base4 + y_at(k)).start()

            if k > 0:
                send()
            else:
                pl.when(y != OWNER)(send)

                @pl.when(y == OWNER)
                def _():
                    pltpu.make_async_copy(fin_out, fin_in, f_recv).start()

    wait_for(fin_in, f_recv)
    pick = (iota((8, SET), 1) == 4 * y + iota((8, SET), 0)).astype(BF16)
    picked = jnp.dot(pick, fin_in[...], preferred_element_type=F32)
    out_ref[...] = picked[:4].astype(BF16)

    @pl.when(is_owner)
    def _():
        for k in range(1, 4):
            wait_for(fin_out, f_send.at[k])
            wait_for(hx_out.at[0], hx_send.at[k])

        @pl.when(y != OWNER)
        def _():
            wait_for(fin_out, f_send.at[0])

    @pl.when(jnp.logical_not(is_owner))
    def _():
        wait_for(rt_out, rt_send.at[0])

    for k in range(1, 4):
        wait_for(rt_out, rt_send.at[k])


def shards(hidden_in, routes, norm_gain, router_weight, gate_weight, up_weight, down_weight):
    dma = pltpu.SemaphoreType.DMA
    any_space = pl.BlockSpec(memory_space=pl.ANY)
    out = pl.pallas_call(
        kernel,
        out_shape=jax.ShapeDtypeStruct((4, CH), BF16),
        in_specs=[any_space] * 7,
        out_specs=pl.BlockSpec(memory_space=pltpu.VMEM),
        scratch_shapes=[
            pltpu.VMEM(hidden_in.shape, BF16),
            pltpu.VMEM(routes.shape, jnp.int32),
            pltpu.VMEM(norm_gain.shape, F32),
            pltpu.VMEM(router_weight.shape, BF16),
            pltpu.VMEM((2, D, HID), BF16),
            pltpu.VMEM((2, D, HID), BF16),
            pltpu.VMEM((2, HID, D), BF16),
            pltpu.VMEM((SET, 128), F32),
            pltpu.VMEM((4, 4, SET, 128), F32),
            pltpu.VMEM((4, SET, 128), F32),
            pltpu.VMEM((4, SET, CH), BF16),
            pltpu.VMEM((4, SET, CH), BF16),
            pltpu.VMEM((STEPS, SET, 64), BF16),
            pltpu.VMEM((SET, CH), F32),
            pltpu.VMEM((EXPERTS, ROWS, CH), BF16),
            pltpu.VMEM((2, 4, 2, EXPERTS, ROWS, CH), BF16),
            pltpu.VMEM((4, 2, 64, CH), BF16),
            pltpu.VMEM((2, 8, 64, CH), BF16),
            pltpu.VMEM((128, 128), F32),
            pltpu.VMEM((EXPERTS, ROWS, CH + 128), BF16),
            pltpu.VMEM((EXPERTS, ROWS, CH + 128), BF16),
            pltpu.VMEM((SET, CH), BF16),
            pltpu.VMEM((SET, CH), BF16),
            dma((2,)),
            dma((2, 5)),
            dma((4,)),
            dma((4, 4)),
            dma((4,)),
            dma((4,)),
            dma((8,)),
            dma((2, 8)),
            dma((7, GROUPS)),
            dma((2, 8, GROUPS)),
            dma((7,)),
            dma((2, 8)),
            dma((8,)),
            dma((8,)),
            dma((4,)),
            dma,
        ],
        compiler_params=pltpu.CompilerParams(
            collective_id=0, has_side_effects=True, vmem_limit_bytes=48 << 20
        ),
    )(hidden_in, routes, norm_gain, router_weight, gate_weight, up_weight, down_weight)
    return out[None]


def solution(mesh):
    return jax.shard_map(
        shards,
        mesh=mesh,
        in_specs=(
            P(None, "expert", None),
            P(None, "section", None, "expert", None),
            P(None, "section", None),
            P(None, "section", None, None),
            P(None, "section", "expert", None, None),
            P(None, "section", "expert", None, None),
            P(None, "section", "expert", None, None),
        ),
        out_specs=P(None, "expert", "section"),
        check_vma=False,
    )
```

time: 651 us -> 252 us (0.39); the launches traced: 641 us -> 251 us
  blocking collectives: 336 us -> 0 us
  Pallas kernels: 0 us -> 245 us
  waiting for transfers between devices: 155 us -> 0 us
  starting transfers between devices: 71.3 us -> 0 us
  matrix products: 47.7 us -> 0 us
  local copies, waits for them, and re-layouts: 19.4 us -> 6.59 us
  other arithmetic: 11.1 us -> 0 us
    all_to_all x11 -> x0, blocking collectives: 336 us -> none  [the longest x8 266 us: lane_layer(): lax.all_to_all(outgoing, 'expert', split_axis=1, concat_axis=1, tiled=True)]
    pallas_call x0 -> x1, Pallas kernels: none -> 245 us  [shards(): pl.pallas_call(kernel, out_shape=jax.ShapeDtypeStruct((4, CH), BF16), in_...]
    all_to_all x6 -> x0, waiting for transfers between devices: 147 us -> none  [finish_rows(): lax.all_to_all(partial_out, 'expert', split_axis=1, concat_axis=1, tiled=...]
    dot_general x40 -> x0, matrix products: 47.7 us -> none  [the longest x8 25.9 us: finish_rows(): jnp.einsum('lrh,lhd->lrd', hidden_acts, w_down, preferred_element_type=jn...]
    all_to_all x6 -> x0, starting transfers between devices: 40.4 us -> none  [finish_rows(): lax.all_to_all(partial_out, 'expert', split_axis=1, concat_axis=1, tiled=...]
    ppermute x7 -> x0, starting transfers between devices: 30.9 us -> none  [passed_along(): return lax.ppermute(x, axis, pairs)]
    reduce_sum x33 -> x0, other arithmetic: 10.1 us -> none  [the longest x8 6.26 us: lane_layer(): jnp.sum(returned.reshape(lane_count, expert_count, slice_count, capacity,...]
    reshape x9 -> x0, local copies, waits for them, and re-layouts: 9.04 us -> none  [the longest x8 8.33 us: finish_rows(): partial_out.reshape(lane_count, device_count, slot_count, model_width)]
  transfers between devices with their start and end apart: 13 -> 0, of which waited for: 12 -> 0; matrix products, arithmetic and copies ran while one was open for 1% -> 0% of each run, Pallas kernels for 0% -> 0%
where the time goes in v1:
time: 252 us; the launch traced here: 251 us
  Pallas kernels  245 us (97%)
  local copies, waits for them, and re-layouts  6.59 us (3%)
    pallas_call x1, Pallas kernels, shards(): pl.pallas_call(kernel, out_shape=jax.ShapeDtypeStruct((4, CH), BF16), in_...  245 us
    unnamed x9, local copies, waits for them, and re-layouts  6.59 us

profile of v1, /device:TPU:1, one launch (start us, length us, event | category | flops | bytes accessed | tf_op | source)
XLA Modules:
  0.0 251.4 jit_solution(5759782030783761201)
XLA Ops:
  0.0 0.8 copy.8.routes_hbm
  0.8 1.7 copy.9.router_hbm
  2.5 0.0 copy-start
  2.5 2.0 copy-done
  4.5 0.0 copy-start.1
  4.5 0.7 copy-done.1
  5.3 0.0 copy-start.2
  5.3 0.7 copy-done.2
  6.0 244.8 %shard_map.73 = bf16[4,896]{1,0:T(4,128)(2,1)S(1)} custom-call(bf16[1,4,3584]{2,1,0:T(4,128)(2,1)S(1)} %copy-done.1, s32[2,1,1,4,2]{4,3,2,1,0:T(4,128)S(1)} %copy.8.routes_hbm, f32[2,1,3584]{2,1,0:T(1,128)S(1)} %copy-done.2, bf16[2,1,3584,8]{3,2,1,0:T(8,128)(2,1)S(1)} %copy.9.router_hbm, bf16[2,1,1,3584,256]{4,3,2,1,0:T(8,128)(2,1)S(1)} %copy-done, ...), custom_call_target="tpu_custom_call" | custom-call | tf_op jit(solution)/shard_map/pallas_call | solution.py:420
  250.8 0.6 copy.11
Async XLA Ops:
  2.5 2.0 copy-start
  4.5 0.7 copy-start.1
  5.3 0.7 copy-start.2

commit v2 on v1

v2 whole, which is shorter than its diff:
```python
import jax
import jax.numpy as jnp
from jax import lax
from jax.experimental import pallas as pl
from jax.experimental.pallas import tpu as pltpu
from jax.sharding import PartitionSpec as P

MESH = pl.DeviceIdType.MESH
F32 = jnp.float32
BF16 = jnp.bfloat16

D = 3584
CH = 896
WIDE = CH + 128
HID = 256
EXPERTS = 8
ROWS = 8
SET = 16
STEPS = 8
FIRST = 3
SECOND = 0
AWAY = (4, 3, -3, 2, -2, 1, -1, 0)
FAR = 3
NEAR = len(AWAY) - FAR
FAR_SLOTS = 2 * FAR
SLOTS = FAR_SLOTS + 8 * NEAR
FAR_ROWS = 16 * FAR


def remote(src, dst, send, recv, section, expert):
    return pltpu.make_async_remote_copy(
        src_ref=src,
        dst_ref=dst,
        send_sem=send,
        recv_sem=recv,
        device_id=(section, expert),
        device_id_type=MESH,
    )


def wait_for(ref, sem):
    pltpu.make_async_copy(ref, ref, sem).wait()


def iota(shape, dim):
    return lax.broadcasted_iota(jnp.int32, shape, dim)


def kernel(
    hidden_hbm, routes_hbm, gain_hbm, router_hbm, gate_hbm, up_hbm, down_hbm, out_ref,
    hid_v, routes_v, gain_v, router_v, gate_v, up_v, down_v,
    rt_out, rt_in, rsum, hx_out, hx_in, place_pt, mix_pt, x_v, x_out, x_in, disp, xb,
    sb, rb, aff_v, near_out, far_out, ro, fin_out, fin_in,
    in_sem, w_sem, rt_send, rt_recv, hx_send, hx_recv, x_send, x_recv, d_send, a_recv,
    g_send, r_send, r_recv, n_send, c_send, c_recv, f_send, f_recv,
):
    s = lax.axis_index("section")
    i = lax.axis_index("expert")
    xh = i // 32
    z = (i // 4) % 8
    y = i % 4
    base4 = i - y
    is_first = s == FIRST
    is_second = s == SECOND

    def y_at(k):
        return (y + k) % 4

    def column(xf, away):
        return ((xh + xf) % 2) * 32 + ((z + away + 8) % 8) * 4

    def expert_at(xf, away):
        return ((xh + xf) % 2) * 4 + ((z + away + 8) % 8) // 2

    small = [
        pltpu.make_async_copy(hidden_hbm, hid_v, in_sem.at[0]),
        pltpu.make_async_copy(routes_hbm, routes_v, in_sem.at[1]),
    ]
    for copy in small:
        copy.start()

    def weights(c):
        return [
            pltpu.make_async_copy(gain_hbm.at[c], gain_v.at[c], w_sem.at[c, 0]),
            pltpu.make_async_copy(router_hbm.at[c], router_v.at[c], w_sem.at[c, 1]),
            pltpu.make_async_copy(gate_hbm.at[c, 0, 0], gate_v.at[c], w_sem.at[c, 2]),
            pltpu.make_async_copy(up_hbm.at[c, 0, 0], up_v.at[c], w_sem.at[c, 3]),
            pltpu.make_async_copy(down_hbm.at[c, 0, 0], down_v.at[c], w_sem.at[c, 4]),
        ]

    for c in range(2):
        for copy in weights(c):
            copy.start()

    barrier = pltpu.get_barrier_semaphore()

    def greet(section, expert):
        pl.semaphore_signal(barrier, inc=1, device_id=(section, expert), device_id_type=MESH)

    def greet_all(section, sign):
        for n, away in enumerate(AWAY):
            for xf in range(2):
                for k in range(1 if n < FAR else 4):
                    greet(section, column(xf, sign * away) + y_at(k))

    for k in range(1, 4):
        greet(s, base4 + y_at(k))
    pl.when(s != FIRST)(lambda: greet_all(FIRST, 1))
    pl.when(s != SECOND)(lambda: greet_all(SECOND, 1))
    pairs = 2 * FAR + 8 * NEAR

    @pl.when(jnp.logical_or(is_first, is_second))
    def _():
        lowest = jnp.where(is_first, 0, 1)
        for n in range(3):
            greet_all(lowest + n, -1)
        pl.semaphore_wait(barrier, 3 + 4 * pairs)

    @pl.when(jnp.logical_not(jnp.logical_or(is_first, is_second)))
    def _():
        pl.semaphore_wait(barrier, 3 + 2 * pairs)

    for copy in small:
        copy.wait()
    place = (iota((SET, 4), 0) == 4 * y + iota((SET, 4), 1)).astype(BF16)

    @pl.when(is_first)
    def _():
        placed = jnp.dot(place, hid_v[0], preferred_element_type=F32).astype(BF16)
        for k in range(4):
            hx_out[k] = placed[:, k * CH : (k + 1) * CH]
        for k in (2, 1, 3):
            remote(
                hx_out.at[y_at(k)], hx_in.at[y], hx_send.at[k], hx_recv.at[y],
                s, base4 + y_at(k),
            ).start()

    lane = iota((4, 128), 1)
    diagonal = iota((4, 4), 0) == iota((4, 4), 1)
    tile = jnp.zeros((4, 128), F32)
    for c in range(2):
        chosen = routes_v[c, 0, 0].astype(F32)
        for k in range(2):
            column_k = jnp.sum(jnp.where(diagonal, chosen[k : k + 1], 0.0), axis=1, keepdims=True)
            tile = tile + jnp.where(lane == 2 * c + k, column_k, 0.0)
    rt_out[...] = jnp.dot(place, tile.astype(BF16), preferred_element_type=F32)

    def send_routes(n, holder, k):
        remote(
            rt_out, rt_in.at[s, y], rt_send.at[n, k], rt_recv.at[s, y],
            holder, base4 + y_at(k),
        ).start()

    for n, holder in enumerate((FIRST, SECOND)):
        for k in range(1, 4):
            send_routes(n, holder, k)
        pl.when(s != holder)(lambda: send_routes(n, holder, 0))
        @pl.when(s == holder)
        def _():
            rt_in[holder, y] = rt_out[...]

    def gather_routes(sec):
        for k in range(1, 4):
            wait_for(rt_in.at[sec, y_at(k)], rt_recv.at[sec, y_at(k)])
        pl.when(s != sec)(lambda: wait_for(rt_in.at[sec, y], rt_recv.at[sec, y]))
        total = jnp.zeros((SET, 128), F32)
        for k in range(4):
            total = total + rt_in[sec, k]
        rsum[sec] = total

    def live_of(step):
        return jnp.where(step < 4, step, 7 - step)

    def placement(step, expert, row):
        half = step // 4
        routes = rsum[live_of(step)]
        lanes = iota((SET, 128), 1)
        one = jnp.sum(jnp.where(lanes == 2 * half, routes, 0.0), axis=1, keepdims=True)
        two = jnp.sum(jnp.where(lanes == 2 * half + 1, routes, 0.0), axis=1, keepdims=True)
        expert = expert.astype(F32)
        named = jnp.logical_or(one == expert, two == expert)
        onehot = jnp.where(named, 1.0, 0.0)
        token = iota((SET, SET), 0)
        other = iota((SET, SET), 1)
        earlier = jnp.logical_and(token // 4 == other // 4, other < token)
        count = jnp.dot(
            jnp.where(earlier, 1.0, 0.0).astype(BF16), onehot.astype(BF16),
            preferred_element_type=F32,
        )
        fits = jnp.logical_and(
            count == (row % 2).astype(F32), row // 2 == iota(row.shape, 0) // 4
        )
        return jnp.where(jnp.logical_and(named, fits), 1.0, 0.0).astype(BF16)

    def make_place(step):
        at = iota((SET, EXPERTS * ROWS), 1)
        place_pt[step] = placement(step, at // ROWS, at % ROWS)

    def make_mix(step):
        at = iota((SET, SLOTS * ROWS), 1)
        slot = at // ROWS
        near = slot >= FAR_SLOTS
        pair = jnp.where(near, FAR_SLOTS + (slot - FAR_SLOTS) // 4, slot)
        n = pair // 2
        away = jnp.zeros(at.shape, jnp.int32)
        for m, value in enumerate(AWAY):
            away = jnp.where(n == m, value, away)
        expert = ((xh + pair % 2) % 2) * 4 + ((z - away + 8) % 8) // 2
        mix_pt[step] = placement(step, expert, at % ROWS)

    def make_all():
        def body(step, carry):
            make_place(step)
            make_mix(step)
            return carry

        lax.fori_loop(0, STEPS, body, 0)

    @pl.when(is_first)
    def _():
        gather_routes(0)
        make_place(0)
        for k in range(1, 4):
            wait_for(hx_in.at[y_at(k)], hx_recv.at[y_at(k)])
        hx_in[y] = hx_out[y]
        x = jnp.zeros((SET, CH), F32)
        for k in range(4):
            x = x + hx_in[k].astype(F32)
        x_v[...] = x

    def combine(step):
        for k in range(SLOTS):
            wait_for(ro.at[k], c_recv.at[k])
        rows = ro[...].astype(F32).reshape(SLOTS * ROWS, WIDE).astype(BF16)
        mixed = jnp.dot(mix_pt[step], rows, preferred_element_type=F32)
        weight = mixed[:, CH : CH + 1] + mixed[:, CH + 1 : CH + 2]
        fresh = x_v[...] + 20.0 * mixed[:, :CH] / weight
        x_v[...] = fresh.astype(BF16).astype(F32)

    def sends(n):
        if n < FAR:
            return [(xf, 0, 2 * n + xf) for xf in (1, 0)]
        return [
            (xf, k, FAR_SLOTS + (2 * (n - FAR) + xf) * 4 + k) for k in (2, 1, 3, 0) for xf in (1, 0)
        ]

    def wait_dispatch():
        for m in range(SLOTS):
            wait_for(disp.at[0], d_send.at[m])

    def holder_step(step):
        half = step // 4

        @pl.when(jnp.logical_or(step == 2, step == 6))
        def _():
            wait_for(x_in, x_recv)
            x_v[...] = x_in[...].astype(F32)

        pl.when(step > 0)(lambda: combine(step - 1))
        pl.when(jnp.logical_and(step != 0, step != 2))(wait_dispatch)
        x_out[...] = x_v[...].astype(BF16)
        rows = lax.dot_general(
            place_pt[step], x_out[...], (((0,), (0,)), ((), ())), preferred_element_type=F32
        )
        disp[...] = rows.reshape(EXPERTS, ROWS, CH).astype(BF16)
        for n, away in enumerate(AWAY):
            for xf, k, m in sends(n):
                remote(
                    disp.at[expert_at(xf, -away)], xb.at[half, y, n, xf],
                    d_send.at[m], a_recv.at[half, y, n],
                    live_of(step), column(xf, -away) + y_at(k),
                ).start()

        @pl.when(jnp.logical_or(step == 1, step == 5))
        def _():
            handed = remote(x_out, x_in, x_send, x_recv, FIRST + SECOND - s, i)
            handed.start()
            handed.wait_send()

        @pl.when(step == 0)
        def _():
            for sec in range(1, 4):
                gather_routes(sec)
            make_all()

    def live_step(half, holder):
        for n in reversed(range(FAR)):
            rows = xb.at[half, y, n]
            wait_for(rows, a_recv.at[half, y, n])
            for k in (2, 1, 3):
                remote(
                    rows, rows, g_send.at[n, k], a_recv.at[half, y, n], s, base4 + y_at(k)
                ).start()
        for copy in weights(half):
            copy.wait()
        gate = jnp.zeros((128, HID), F32)
        up = jnp.zeros((128, HID), F32)
        logits = jnp.zeros((128, EXPERTS), F32)
        squares = jnp.zeros((128, 1), F32)
        for k in (0, 1, 3, 2):
            yk = y_at(k)
            for n in range(FAR if k == 0 else 0, len(AWAY)):
                wait_for(xb.at[half, yk, n], a_recv.at[half, yk, n])
            rows = xb[half, yk].astype(F32).reshape(128, CH)
            squares = squares + jnp.sum(rows * rows, axis=1, keepdims=True)
            start = pl.multiple_of(yk * CH, 128)
            depth = pl.ds(start, CH)
            scaled = (rows * gain_v[half, :, depth]).astype(BF16)
            gate = gate + jnp.dot(scaled, gate_v[half, depth, :], preferred_element_type=F32)
            up = up + jnp.dot(scaled, up_v[half, depth, :], preferred_element_type=F32)
            logits = logits + lax.dot_general(
                scaled, router_v[half, 0, :, depth], (((1,), (1,)), ((), ())),
                preferred_element_type=F32,
            )
        scale = lax.rsqrt(squares * (1.0 / D) + 1e-06)
        gate = gate * scale
        act = (gate * jax.nn.sigmoid(gate) * (up * scale)).astype(BF16)
        own = jnp.where(iota((128, EXPERTS), 1) == i // 8, logits, 0.0)
        affinity = jax.nn.sigmoid(jnp.sum(own, axis=1, keepdims=True) * scale)
        high = affinity.astype(BF16).astype(F32)
        lanes = iota((128, 128), 1)
        extra = jnp.where(lanes == 0, high, jnp.where(lanes == 1, affinity - high, 0.0))
        aff_v[...] = jnp.broadcast_to(affinity, (128, 128))
        near_extra = extra[FAR_ROWS:].reshape(2 * NEAR, ROWS, 128).astype(BF16)
        far_out[:, :, CH:] = (4.0 * extra[:FAR_ROWS]).reshape(FAR_SLOTS, ROWS, 128).astype(BF16)

        for k in (2, 1, 3, 0):
            yk = y_at(k)
            cols = pl.ds(pl.multiple_of(yk * CH, 128), CH)
            piece = jnp.dot(act, down_v[half, :, cols], preferred_element_type=F32)
            sb[yk] = piece[:FAR_ROWS].reshape(FAR, 16, CH).astype(BF16)
            weighted = piece[FAR_ROWS:] * affinity[FAR_ROWS:]
            near_out[yk, :, :, :CH] = weighted.reshape(2 * NEAR, ROWS, CH).astype(BF16)
            near_out[yk, :, :, CH:] = near_extra
        for n in range(FAR):
            for k in (2, 1, 3):
                remote(
                    sb.at[y_at(k), n], rb.at[half, y, n], r_send.at[n, k],
                    r_recv.at[half, y, n], s, base4 + y_at(k),
                ).start()
        for n in range(FAR, len(AWAY)):
            for xf, k, m in sends(n):
                pair = 2 * (n - FAR) + xf
                remote(
                    near_out.at[y_at(k), pair], ro.at[FAR_SLOTS + pair * 4 + y],
                    n_send.at[m - FAR_SLOTS], c_recv.at[FAR_SLOTS + pair * 4 + y],
                    holder, column(xf, AWAY[n]) + y_at(k),
                ).start()
        for n in range(FAR):
            total = sb[y, n].astype(F32)
            for k in (1, 3, 2):
                wait_for(rb.at[half, y_at(k), n], r_recv.at[half, y_at(k), n])
                total = total + rb[half, y_at(k), n].astype(F32)
            total = total * aff_v[16 * n : 16 * n + 16, :1]
            far_out[2 * n : 2 * n + 2, :, :CH] = total.reshape(2, ROWS, CH).astype(BF16)
            for xf, k, m in sends(n):
                remote(
                    far_out.at[m], ro.at[m], c_send.at[m], c_recv.at[m],
                    holder, column(xf, AWAY[n]) + y,
                ).start()

        for n in range(FAR):
            for k in range(1, 4):
                wait_for(xb.at[half, y, n], g_send.at[n, k])
                wait_for(sb.at[0, 0], r_send.at[n, k])
        for m in range(FAR_SLOTS):
            wait_for(far_out.at[m], c_send.at[m])
        for m in range(SLOTS - FAR_SLOTS):
            wait_for(near_out.at[0, 0], n_send.at[m])

    def holder_of(step):
        return jnp.where(jnp.logical_and(step > 1, step < 6), SECOND, FIRST)

    def one_step(step, carry):
        pl.when(s == holder_of(step))(lambda: holder_step(step))

        @pl.when(jnp.logical_and(is_second, step == 1))
        def _():
            for sec in range(4):
                gather_routes(sec)
            make_all()

        pl.when(s == live_of(step))(lambda: live_step(step // 4, holder_of(step + 1)))
        return carry

    lax.fori_loop(0, STEPS, one_step, 0)
    pl.when(is_second)(wait_dispatch)

    @pl.when(is_first)
    def _():
        combine(STEPS - 1)
        fin_out[...] = x_v[...].astype(BF16)

        def send_last(k):
            remote(fin_out, fin_in, f_send.at[k], f_recv, y, base4 + y_at(k)).start()

        for k in (2, 1, 3):
            send_last(k)
        pl.when(y != FIRST)(lambda: send_last(0))

        @pl.when(y == FIRST)
        def _():
            pltpu.make_async_copy(fin_out, fin_in, f_recv).start()

    wait_for(fin_in, f_recv)
    pick = (iota((8, SET), 1) == 4 * y + iota((8, SET), 0)).astype(BF16)
    picked = jnp.dot(pick, fin_in[...], preferred_element_type=F32)
    out_ref[...] = picked[:4].astype(BF16)

    @pl.when(is_first)
    def _():
        wait_dispatch()
        for k in range(1, 4):
            wait_for(fin_out, f_send.at[k])
            wait_for(hx_out.at[0], hx_send.at[k])
        pl.when(y != FIRST)(lambda: wait_for(fin_out, f_send.at[0]))

    for n, holder in enumerate((FIRST, SECOND)):
        for k in range(1, 4):
            wait_for(rt_out, rt_send.at[n, k])
        pl.when(s != holder)(lambda: wait_for(rt_out, rt_send.at[n, 0]))


def shards(hidden_in, routes, norm_gain, router_weight, gate_weight, up_weight, down_weight):
    routes = jnp.swapaxes(routes, 3, 4)
    router_weight = jnp.swapaxes(router_weight, 2, 3)
    dma = pltpu.SemaphoreType.DMA
    in_hbm = pl.BlockSpec(memory_space=pltpu.HBM)
    out = pl.pallas_call(
        kernel,
        out_shape=jax.ShapeDtypeStruct((4, CH), BF16),
        in_specs=[in_hbm] * 7,
        out_specs=pl.BlockSpec(memory_space=pltpu.VMEM),
        scratch_shapes=[
            pltpu.VMEM(hidden_in.shape, BF16),
            pltpu.VMEM(routes.shape, jnp.int32),
            pltpu.VMEM(norm_gain.shape, F32),
            pltpu.VMEM(router_weight.shape, BF16),
            pltpu.VMEM((2, D, HID), BF16),
            pltpu.VMEM((2, D, HID), BF16),
            pltpu.VMEM((2, HID, D), BF16),
            pltpu.VMEM((SET, 128), F32),
            pltpu.VMEM((4, 4, SET, 128), F32),
            pltpu.VMEM((4, SET, 128), F32),
            pltpu.VMEM((4, SET, CH), BF16),
            pltpu.VMEM((4, SET, CH), BF16),
            pltpu.VMEM((STEPS, SET, EXPERTS * ROWS), BF16),
            pltpu.VMEM((STEPS, SET, SLOTS * ROWS), BF16),
            pltpu.VMEM((SET, CH), F32),
            pltpu.VMEM((SET, CH), BF16),
            pltpu.VMEM((SET, CH), BF16),
            pltpu.VMEM((EXPERTS, ROWS, CH), BF16),
            pltpu.VMEM((2, 4, len(AWAY), 2, ROWS, CH), BF16),
            pltpu.VMEM((4, FAR, 16, CH), BF16),
            pltpu.VMEM((2, 4, FAR, 16, CH), BF16),
            pltpu.VMEM((128, 128), F32),
            pltpu.VMEM((4, 2 * NEAR, ROWS, WIDE), BF16),
            pltpu.VMEM((FAR_SLOTS, ROWS, WIDE), BF16),
            pltpu.VMEM((SLOTS, ROWS, WIDE), BF16),
            pltpu.VMEM((SET, CH), BF16),
            pltpu.VMEM((SET, CH), BF16),
            dma((2,)),
            dma((2, 5)),
            dma((2, 4)),
            dma((4, 4)),
            dma((4,)),
            dma((4,)),
            dma,
            dma,
            dma((SLOTS,)),
            dma((2, 4, len(AWAY))),
            dma((FAR, 4)),
            dma((FAR, 4)),
            dma((2, 4, FAR)),
            dma((8 * NEAR,)),
            dma((FAR_SLOTS,)),
            dma((SLOTS,)),
            dma((4,)),
            dma,
        ],
        compiler_params=pltpu.CompilerParams(
            collective_id=0, has_side_effects=True, vmem_limit_bytes=63 << 20
        ),
    )(hidden_in, routes, norm_gain, router_weight, gate_weight, up_weight, down_weight)
    return out[None]


def solution(mesh):
    return jax.shard_map(
        shards,
        mesh=mesh,
        in_specs=(
            P(None, "expert", None),
            P(None, "section", None, "expert", None),
            P(None, "section", None),
            P(None, "section", None, None),
            P(None, "section", "expert", None, None),
            P(None, "section", "expert", None, None),
            P(None, "section", "expert", None, None),
        ),
        out_specs=P(None, "expert", "section"),
        check_vma=False,
    )
```

time: 252 us -> 212 us (0.84)
  Pallas kernels: 245 us -> 211 us
  local copies, waits for them, and re-layouts: 6.59 us -> 1.29 us
    pallas_call x1, Pallas kernels: 245 us -> 211 us  [shards(): pl.pallas_call(kernel, out_shape=jax.ShapeDtypeStruct((4, CH), BF16), in_...]
    unnamed x9 -> x1, local copies, waits for them, and re-layouts: 6.59 us -> 1.29 us
where the time goes in v2:
time: 212 us
  Pallas kernels  211 us (100%)
    pallas_call x1, Pallas kernels, shards(): pl.pallas_call(kernel, out_shape=jax.ShapeDtypeStruct((4, CH), BF16), in_...  211 us

profile of v2, /device:TPU:1, one launch (start us, length us, event | category | flops | bytes accessed | tf_op | source)
XLA Modules:
  0.0 212.2 jit_solution(12106170418728227853)
XLA Ops:
  0.0 210.9 %shard_map.73 = bf16[4,896]{1,0:T(4,128)(2,1)} custom-call(bf16[1,4,3584]{2,1,0:T(4,128)(2,1)} %hidden_hbm.1, s32[2,1,1,2,4]{4,3,2,1,0:T(2,128)} %bitcast.5, f32[2,1,3584]{2,1,0:T(1,128)} %gain_hbm.1, bf16[2,1,8,3584]{3,2,1,0:T(8,128)(2,1)} %bitcast.3, bf16[2,1,1,3584,256]{4,3,2,1,0:T(8,128)(2,1)} %gate_hbm.1, bf16[2,1,1,3584,256]{4,3,2,1,0:T(8,128)(2,1)} %up_hbm.1, ...), custom_call_target="tpu_custom_call" | custom-call | tf_op jit(solution)/shard_map/pallas_call | solution.py:429
  210.9 1.3 copy.9

commit v3 on v2

--- a/solution.py
+++ b/solution.py
@@ -49,8 +49,8 @@
 def kernel(
     hidden_hbm, routes_hbm, gain_hbm, router_hbm, gate_hbm, up_hbm, down_hbm, out_ref,
     hid_v, routes_v, gain_v, router_v, gate_v, up_v, down_v,
-    rt_out, rt_in, rsum, hx_out, hx_in, place_pt, mix_pt, x_v, x_out, x_in, disp, xb,
-    sb, rb, aff_v, near_out, far_out, ro, fin_out, fin_in,
+    rt_out, rt_in, rsum, hx_out, hx_in, place_pt, far_pt, near_pt, x_v, x_out, x_in, disp, xb,
+    own_router, sb, rb, near_out, far_out, ro, fin_out, fin_in,
     in_sem, w_sem, rt_send, rt_recv, hx_send, hx_recv, x_send, x_recv, d_send, a_recv,
     g_send, r_send, r_recv, n_send, c_send, c_recv, f_send, f_recv,
 ):
@@ -91,6 +91,8 @@
     for c in range(2):
         for copy in weights(c):
             copy.start()
+
+    ro[:, :, CH:] = jnp.zeros((SLOTS, ROWS, 128), BF16)
 
     barrier = pltpu.get_barrier_semaphore()
 
@@ -196,9 +198,9 @@
         at = iota((SET, EXPERTS * ROWS), 1)
         place_pt[step] = placement(step, at // ROWS, at % ROWS)
 
-    def make_mix(step):
-        at = iota((SET, SLOTS * ROWS), 1)
-        slot = at // ROWS
+    def make_mix(step, first, count):
+        at = iota((SET, count * ROWS), 1)
+        slot = first + at // ROWS
         near = slot >= FAR_SLOTS
         pair = jnp.where(near, FAR_SLOTS + (slot - FAR_SLOTS) // 4, slot)
         n = pair // 2
@@ -206,12 +208,13 @@
         for m, value in enumerate(AWAY):
             away = jnp.where(n == m, value, away)
         expert = ((xh + pair % 2) % 2) * 4 + ((z - away + 8) % 8) // 2
-        mix_pt[step] = placement(step, expert, at % ROWS)
+        return placement(step, expert, at % ROWS)
 
     def make_all():
         def body(step, carry):
             make_place(step)
-            make_mix(step)
+            far_pt[step] = make_mix(step, 0, FAR_SLOTS)
+            near_pt[step] = make_mix(step, FAR_SLOTS, SLOTS - FAR_SLOTS)
             return carry
 
         lax.fori_loop(0, STEPS, body, 0)
@@ -229,10 +232,13 @@
         x_v[...] = x
 
     def combine(step):
-        for k in range(SLOTS):
-            wait_for(ro.at[k], c_recv.at[k])
-        rows = ro[...].astype(F32).reshape(SLOTS * ROWS, WIDE).astype(BF16)
-        mixed = jnp.dot(mix_pt[step], rows, preferred_element_type=F32)
+        widths = [WIDE] * FAR_SLOTS + [WIDE, CH, CH, CH] * (2 * NEAR)
+        mixed = jnp.zeros((SET, WIDE), F32)
+        for matrix, first, last in ((near_pt, FAR_SLOTS, SLOTS), (far_pt, 0, FAR_SLOTS)):
+            for k in range(first, last):
+                wait_for(ro.at[k, :, pl.ds(0, widths[k])], c_recv.at[k])
+            rows = ro[first:last].astype(F32).reshape((last - first) * ROWS, WIDE).astype(BF16)
+            mixed = mixed + jnp.dot(matrix[step], rows, preferred_element_type=F32)
         weight = mixed[:, CH : CH + 1] + mixed[:, CH + 1 : CH + 2]
         fresh = x_v[...] + 20.0 * mixed[:, :CH] / weight
         x_v[...] = fresh.astype(BF16).astype(F32)
@@ -263,13 +269,16 @@
             place_pt[step], x_out[...], (((0,), (0,)), ((), ())), preferred_element_type=F32
         )
         disp[...] = rows.reshape(EXPERTS, ROWS, CH).astype(BF16)
-        for n, away in enumerate(AWAY):
-            for xf, k, m in sends(n):
-                remote(
-                    disp.at[expert_at(xf, -away)], xb.at[half, y, n, xf],
-                    d_send.at[m], a_recv.at[half, y, n],
-                    live_of(step), column(xf, -away) + y_at(k),
-                ).start()
+        order = [(n,) + t for n in range(FAR) for t in sends(n)]
+        near = [(n,) + t for n in range(FAR, len(AWAY)) for t in sends(n)]
+        order += sorted(near, key=lambda t: (2, 1, 3, 0).index(t[2]))
+        for n, xf, k, m in order:
+            away = AWAY[n]
+            remote(
+                disp.at[expert_at(xf, -away)], xb.at[half, y, n, xf],
+                d_send.at[m], a_recv.at[half, y, n],
+                live_of(step), column(xf, -away) + y_at(k),
+            ).start()
 
         @pl.when(jnp.logical_or(step == 1, step == 5))
         def _():
@@ -284,6 +293,12 @@
             make_all()
 
     def live_step(half, holder):
+        for copy in weights(half):
+            copy.wait()
+        own = iota((EXPERTS, D), 0) == i // 8
+        own_router[...] = jnp.sum(
+            jnp.where(own, router_v[half, 0].astype(F32), 0.0), axis=0, keepdims=True
+        )
         for n in reversed(range(FAR)):
             rows = xb.at[half, y, n]
             wait_for(rows, a_recv.at[half, y, n])
@@ -291,67 +306,73 @@
                 remote(
                     rows, rows, g_send.at[n, k], a_recv.at[half, y, n], s, base4 + y_at(k)
                 ).start()
-        for copy in weights(half):
-            copy.wait()
-        gate = jnp.zeros((128, HID), F32)
-        up = jnp.zeros((128, HID), F32)
-        logits = jnp.zeros((128, EXPERTS), F32)
-        squares = jnp.zeros((128, 1), F32)
-        for k in (0, 1, 3, 2):
-            yk = y_at(k)
-            for n in range(FAR if k == 0 else 0, len(AWAY)):
-                wait_for(xb.at[half, yk, n], a_recv.at[half, yk, n])
-            rows = xb[half, yk].astype(F32).reshape(128, CH)
-            squares = squares + jnp.sum(rows * rows, axis=1, keepdims=True)
-            start = pl.multiple_of(yk * CH, 128)
-            depth = pl.ds(start, CH)
-            scaled = (rows * gain_v[half, :, depth]).astype(BF16)
-            gate = gate + jnp.dot(scaled, gate_v[half, depth, :], preferred_element_type=F32)
-            up = up + jnp.dot(scaled, up_v[half, depth, :], preferred_element_type=F32)
-            logits = logits + lax.dot_general(
-                scaled, router_v[half, 0, :, depth], (((1,), (1,)), ((), ())),
-                preferred_element_type=F32,
-            )
-        scale = lax.rsqrt(squares * (1.0 / D) + 1e-06)
-        gate = gate * scale
-        act = (gate * jax.nn.sigmoid(gate) * (up * scale)).astype(BF16)
-        own = jnp.where(iota((128, EXPERTS), 1) == i // 8, logits, 0.0)
-        affinity = jax.nn.sigmoid(jnp.sum(own, axis=1, keepdims=True) * scale)
-        high = affinity.astype(BF16).astype(F32)
-        lanes = iota((128, 128), 1)
-        extra = jnp.where(lanes == 0, high, jnp.where(lanes == 1, affinity - high, 0.0))
-        aff_v[...] = jnp.broadcast_to(affinity, (128, 128))
-        near_extra = extra[FAR_ROWS:].reshape(2 * NEAR, ROWS, 128).astype(BF16)
-        far_out[:, :, CH:] = (4.0 * extra[:FAR_ROWS]).reshape(FAR_SLOTS, ROWS, 128).astype(BF16)
-
+        def hidden(first, last):
+            count = 16 * (last - first)
+            gate = jnp.zeros((count, HID), F32)
+            up = jnp.zeros((count, HID), F32)
+            logits = jnp.zeros((count, 1), F32)
+            squares = jnp.zeros((count, 1), F32)
+            for k in (0, 1, 3, 2):
+                yk = y_at(k)
+                for n in range(first, last):
+                    if k > 0 or n >= FAR:
+                        wait_for(xb.at[half, yk, n], a_recv.at[half, yk, n])
+                rows = xb[half, yk, first:last].astype(F32).reshape(count, CH)
+                squares = squares + jnp.sum(rows * rows, axis=1, keepdims=True)
+                depth = pl.ds(pl.multiple_of(yk * CH, 128), CH)
+                scaled = (rows * gain_v[half, :, depth]).astype(BF16)
+                gate = gate + jnp.dot(scaled, gate_v[half, depth, :], preferred_element_type=F32)
+                up = up + jnp.dot(scaled, up_v[half, depth, :], preferred_element_type=F32)
+                logits = logits + jnp.sum(
+                    scaled.astype(F32) * own_router[:, depth], axis=1, keepdims=True
+                )
+            scale = lax.rsqrt(squares * (1.0 / D) + 1e-06)
+            gate = gate * scale
+            act = (gate * jax.nn.sigmoid(gate) * (up * scale)).astype(BF16)
+            affinity = jax.nn.sigmoid(logits * scale)
+            high = affinity.astype(BF16).astype(F32)
+            lanes = iota((count, 128), 1)
+            extra = jnp.where(lanes == 0, high, jnp.where(lanes == 1, affinity - high, 0.0))
+            return act, affinity, extra
+
+        def piece_of(act, yk):
+            cols = pl.ds(pl.multiple_of(yk * CH, 128), CH)
+            return jnp.dot(act, down_v[half, :, cols], preferred_element_type=F32)
+
+        act, affinity, extra = hidden(FAR, len(AWAY))
+        near_out[y, :, :, CH:] = (4.0 * extra).reshape(2 * NEAR, ROWS, 128).astype(BF16)
         for k in (2, 1, 3, 0):
             yk = y_at(k)
-            cols = pl.ds(pl.multiple_of(yk * CH, 128), CH)
-            piece = jnp.dot(act, down_v[half, :, cols], preferred_element_type=F32)
-            sb[yk] = piece[:FAR_ROWS].reshape(FAR, 16, CH).astype(BF16)
-            weighted = piece[FAR_ROWS:] * affinity[FAR_ROWS:]
+            weighted = piece_of(act, yk) * affinity
             near_out[yk, :, :, :CH] = weighted.reshape(2 * NEAR, ROWS, CH).astype(BF16)
-            near_out[yk, :, :, CH:] = near_extra
-        for n in range(FAR):
-            for k in (2, 1, 3):
-                remote(
-                    sb.at[y_at(k), n], rb.at[half, y, n], r_send.at[n, k],
-                    r_recv.at[half, y, n], s, base4 + y_at(k),
-                ).start()
-        for n in range(FAR, len(AWAY)):
-            for xf, k, m in sends(n):
-                pair = 2 * (n - FAR) + xf
-                remote(
-                    near_out.at[y_at(k), pair], ro.at[FAR_SLOTS + pair * 4 + y],
-                    n_send.at[m - FAR_SLOTS], c_recv.at[FAR_SLOTS + pair * 4 + y],
-                    holder, column(xf, AWAY[n]) + y_at(k),
-                ).start()
+            for n in range(FAR, len(AWAY)):
+                for xf in (1, 0):
+                    pair = 2 * (n - FAR) + xf
+                    width = pl.ds(0, WIDE if k == 0 else CH)
+                    remote(
+                        near_out.at[yk, pair, :, width],
+                        ro.at[FAR_SLOTS + pair * 4 + k, :, width],
+                        n_send.at[pair * 4 + k], c_recv.at[FAR_SLOTS + pair * 4 + k],
+                        holder, column(xf, AWAY[n]) + yk,
+                    ).start()
+
+        act, affinity, extra = hidden(0, FAR)
+        far_out[:, :, CH:] = (4.0 * extra).reshape(FAR_SLOTS, ROWS, 128).astype(BF16)
+        for k in (2, 1, 3, 0):
+            yk = y_at(k)
+            sb[yk] = piece_of(act, yk).reshape(FAR, 16, CH).astype(BF16)
+            if k > 0:
+                for n in range(FAR):
+                    remote(
+                        sb.at[yk, n], rb.at[half, y, n], r_send.at[n, k],
+                        r_recv.at[half, y, n], s, base4 + yk,
+                    ).start()
         for n in range(FAR):
             total = sb[y, n].astype(F32)
             for k in (1, 3, 2):
                 wait_for(rb.at[half, y_at(k), n], r_recv.at[half, y_at(k), n])
                 total = total + rb[half, y_at(k), n].astype(F32)
-            total = total * aff_v[16 * n : 16 * n + 16, :1]
+            total = total * affinity[16 * n : 16 * n + 16]
             far_out[2 * n : 2 * n + 2, :, :CH] = total.reshape(2, ROWS, CH).astype(BF16)
             for xf, k, m in sends(n):
                 remote(
@@ -366,7 +387,7 @@
         for m in range(FAR_SLOTS):
             wait_for(far_out.at[m], c_send.at[m])
         for m in range(SLOTS - FAR_SLOTS):
-            wait_for(near_out.at[0, 0], n_send.at[m])
+            wait_for(near_out.at[0, 0, :, pl.ds(0, CH if m % 4 else WIDE)], n_send.at[m])
 
     def holder_of(step):
         return jnp.where(jnp.logical_and(step > 1, step < 6), SECOND, FIRST)
@@ -445,15 +466,16 @@
             pltpu.VMEM((4, SET, CH), BF16),
             pltpu.VMEM((4, SET, CH), BF16),
             pltpu.VMEM((STEPS, SET, EXPERTS * ROWS), BF16),
-            pltpu.VMEM((STEPS, SET, SLOTS * ROWS), BF16),
+            pltpu.VMEM((STEPS, SET, FAR_SLOTS * ROWS), BF16),
+            pltpu.VMEM((STEPS, SET, (SLOTS - FAR_SLOTS) * ROWS), BF16),
             pltpu.VMEM((SET, CH), F32),
             pltpu.VMEM((SET, CH), BF16),
             pltpu.VMEM((SET, CH), BF16),
             pltpu.VMEM((EXPERTS, ROWS, CH), BF16),
             pltpu.VMEM((2, 4, len(AWAY), 2, ROWS, CH), BF16),
+            pltpu.VMEM((1, D), F32),
             pltpu.VMEM((4, FAR, 16, CH), BF16),
             pltpu.VMEM((2, 4, FAR, 16, CH), BF16),
-            pltpu.VMEM((128, 128), F32),
             pltpu.VMEM((4, 2 * NEAR, ROWS, WIDE), BF16),
             pltpu.VMEM((FAR_SLOTS, ROWS, WIDE), BF16),
             pltpu.VMEM((SLOTS, ROWS, WIDE), BF16),

time: 212 us -> 207 us (0.976)
  Pallas kernels: 211 us -> 206 us
    pallas_call x1, Pallas kernels: 211 us -> 206 us  [shards(): pl.pallas_call(kernel, out_shape=jax.ShapeDtypeStruct((4, CH), BF16), in_...]
where the time goes in v3:
time: 207 us
  Pallas kernels  206 us (100%)
    pallas_call x1, Pallas kernels, shards(): pl.pallas_call(kernel, out_shape=jax.ShapeDtypeStruct((4, CH), BF16), in_...  206 us

profile of v3, /device:TPU:1, one launch (start us, length us, event | category | flops | bytes accessed | tf_op | source)
XLA Modules:
  0.0 207.1 jit_solution(4191154132615339930)
XLA Ops:
  0.0 205.8 %shard_map.73 = bf16[4,896]{1,0:T(4,128)(2,1)} custom-call(bf16[1,4,3584]{2,1,0:T(4,128)(2,1)} %hidden_hbm.1, s32[2,1,1,2,4]{4,3,2,1,0:T(2,128)} %bitcast.5, f32[2,1,3584]{2,1,0:T(1,128)} %gain_hbm.1, bf16[2,1,8,3584]{3,2,1,0:T(8,128)(2,1)} %bitcast.3, bf16[2,1,1,3584,256]{4,3,2,1,0:T(8,128)(2,1)} %gate_hbm.1, bf16[2,1,1,3584,256]{4,3,2,1,0:T(8,128)(2,1)} %up_hbm.1, ...), custom_call_target="tpu_custom_call" | custom-call | tf_op jit(solution)/shard_map/pallas_call | solution.py:450
  205.8 1.3 copy.9

commit v4 on v3

--- a/solution.py
+++ b/solution.py
@@ -116,11 +116,6 @@
         lowest = jnp.where(is_first, 0, 1)
         for n in range(3):
             greet_all(lowest + n, -1)
-        pl.semaphore_wait(barrier, 3 + 4 * pairs)
-
-    @pl.when(jnp.logical_not(jnp.logical_or(is_first, is_second)))
-    def _():
-        pl.semaphore_wait(barrier, 3 + 2 * pairs)
 
     for copy in small:
         copy.wait()
@@ -131,11 +126,6 @@
         placed = jnp.dot(place, hid_v[0], preferred_element_type=F32).astype(BF16)
         for k in range(4):
             hx_out[k] = placed[:, k * CH : (k + 1) * CH]
-        for k in (2, 1, 3):
-            remote(
-                hx_out.at[y_at(k)], hx_in.at[y], hx_send.at[k], hx_recv.at[y],
-                s, base4 + y_at(k),
-            ).start()
 
     lane = iota((4, 128), 1)
     diagonal = iota((4, 4), 0) == iota((4, 4), 1)
@@ -146,6 +136,16 @@
             column_k = jnp.sum(jnp.where(diagonal, chosen[k : k + 1], 0.0), axis=1, keepdims=True)
             tile = tile + jnp.where(lane == 2 * c + k, column_k, 0.0)
     rt_out[...] = jnp.dot(place, tile.astype(BF16), preferred_element_type=F32)
+
+    pl.semaphore_wait(barrier, 3 + jnp.where(jnp.logical_or(is_first, is_second), 4, 2) * pairs)
+
+    @pl.when(is_first)
+    def _():
+        for k in (2, 1, 3):
+            remote(
+                hx_out.at[y_at(k)], hx_in.at[y], hx_send.at[k], hx_recv.at[y],
+                s, base4 + y_at(k),
+            ).start()
 
     def send_routes(n, holder, k):
         remote(
@@ -262,8 +262,8 @@
             wait_for(x_in, x_recv)
             x_v[...] = x_in[...].astype(F32)
 
+        pl.when(jnp.logical_and(step != 0, step != 2))(wait_dispatch)
         pl.when(step > 0)(lambda: combine(step - 1))
-        pl.when(jnp.logical_and(step != 0, step != 2))(wait_dispatch)
         x_out[...] = x_v[...].astype(BF16)
         rows = lax.dot_general(
             place_pt[step], x_out[...], (((0,), (0,)), ((), ())), preferred_element_type=F32
@@ -339,12 +339,8 @@
             cols = pl.ds(pl.multiple_of(yk * CH, 128), CH)
             return jnp.dot(act, down_v[half, :, cols], preferred_element_type=F32)
 
-        act, affinity, extra = hidden(FAR, len(AWAY))
-        near_out[y, :, :, CH:] = (4.0 * extra).reshape(2 * NEAR, ROWS, 128).astype(BF16)
-        for k in (2, 1, 3, 0):
+        def send_near(k):
             yk = y_at(k)
-            weighted = piece_of(act, yk) * affinity
-            near_out[yk, :, :, :CH] = weighted.reshape(2 * NEAR, ROWS, CH).astype(BF16)
             for n in range(FAR, len(AWAY)):
                 for xf in (1, 0):
                     pair = 2 * (n - FAR) + xf
@@ -355,6 +351,15 @@
                         n_send.at[pair * 4 + k], c_recv.at[FAR_SLOTS + pair * 4 + k],
                         holder, column(xf, AWAY[n]) + yk,
                     ).start()
+
+        act, affinity, extra = hidden(FAR, len(AWAY))
+        near_out[y, :, :, CH:] = (4.0 * extra).reshape(2 * NEAR, ROWS, 128).astype(BF16)
+        for k in (2, 1, 3, 0):
+            yk = y_at(k)
+            weighted = piece_of(act, yk) * affinity
+            near_out[yk, :, :, :CH] = weighted.reshape(2 * NEAR, ROWS, CH).astype(BF16)
+            if k in (2,):
+                send_near(k)
 
         act, affinity, extra = hidden(0, FAR)
         far_out[:, :, CH:] = (4.0 * extra).reshape(FAR_SLOTS, ROWS, 128).astype(BF16)
@@ -367,6 +372,8 @@
                         sb.at[yk, n], rb.at[half, y, n], r_send.at[n, k],
                         r_recv.at[half, y, n], s, base4 + yk,
                     ).start()
+        for k in (1, 3, 0):
+            send_near(k)
         for n in range(FAR):
             total = sb[y, n].astype(F32)
             for k in (1, 3, 2):

time: 207 us -> 204 us (0.986)
  Pallas kernels: 206 us -> 202 us
    pallas_call x1, Pallas kernels: 206 us -> 202 us  [shards(): pl.pallas_call(kernel, out_shape=jax.ShapeDtypeStruct((4, CH), BF16), in_...]
where the time goes in v4:
time: 204 us
  Pallas kernels  202 us (99%)
    pallas_call x1, Pallas kernels, shards(): pl.pallas_call(kernel, out_shape=jax.ShapeDtypeStruct((4, CH), BF16), in_...  202 us

profile of v4, /device:TPU:1, one launch (start us, length us, event | category | flops | bytes accessed | tf_op | source)
XLA Modules:
  0.0 203.8 jit_solution(17948586127945830812)
XLA Ops:
  0.0 202.5 %shard_map.73 = bf16[4,896]{1,0:T(4,128)(2,1)} custom-call(bf16[1,4,3584]{2,1,0:T(4,128)(2,1)} %hidden_hbm.1, s32[2,1,1,2,4]{4,3,2,1,0:T(2,128)} %bitcast.5, f32[2,1,3584]{2,1,0:T(1,128)} %gain_hbm.1, bf16[2,1,8,3584]{3,2,1,0:T(8,128)(2,1)} %bitcast.3, bf16[2,1,1,3584,256]{4,3,2,1,0:T(8,128)(2,1)} %gate_hbm.1, bf16[2,1,1,3584,256]{4,3,2,1,0:T(8,128)(2,1)} %up_hbm.1, ...), custom_call_target="tpu_custom_call" | custom-call | tf_op jit(solution)/shard_map/pallas_call | solution.py:457
  202.5 1.3 copy.9
